TPU v7x, 32 devices: a whole 2x2x4 slice. The times are simulated.
32 devices in a mesh: pipe: 4 (over x, core), expert: 2 (over y), dp: 4 (over z).
Axes of the slice: x: 2, y: 2, z: 4, core: 2. Of those that a mesh axis runs over, the one named last changes fastest.
Arguments:
- inputs: bfloat16 [4, 1024, 4096], P('pipe', ('expert', 'dp')), may hold values from -6 to 6
- routes: int32 [4, 1024, 1], P('pipe', ('expert', 'dp')), may hold values from 0 to 1; in each aligned block of 128 rows (0 to 127, 128 to 255, ..., all dimensions but the last counted through in order) at most 80 rows name the same one
- router_scores: float32 [4, 1024, 8], P('pipe', ('expert', 'dp')), may hold values from -2 to 2
- cotangent: bfloat16 [4, 1024, 4096], P('pipe', ('expert', 'dp')), may hold values from -6 to 6
- w_gate: bfloat16 [4, 2, 768, 4096], P('pipe', 'expert', 'dp'), may hold values from -0.09375 to 0.09375
- w_up: bfloat16 [4, 2, 768, 4096], P('pipe', 'expert', 'dp'), may hold values from -0.09375 to 0.09375
- w_down: bfloat16 [4, 2, 768, 4096], P('pipe', 'expert', 'dp'), may hold values from -0.21875 to 0.21875
Outputs:
- score_grad: float32 [4, 1024, 8], P('pipe', ('expert', 'dp'))
- grad_prev: bfloat16 [4, 1024, 4096], P('pipe', ('expert', 'dp'))
- grad_gate: bfloat16 [4, 2, 768, 4096], P('pipe', 'expert', 'dp')
- grad_up: bfloat16 [4, 2, 768, 4096], P('pipe', 'expert', 'dp')
- grad_down: bfloat16 [4, 2, 768, 4096], P('pipe', 'expert', 'dp')
Inputs may be any that keep to these rules, and one draw needn't show every extreme that they name: `routes`: among the 128 tokens of one device in one section (one block) no expert is named more than 80 times, and in every draw some block names some expert exactly 80 times. Every expert is named by some token.
All inputs are finite; a program needn't handle non-finite values.
Results may differ from a plain program's by a relative error of at most 0.02.
Values may be sent and summed in bfloat16 or wider, within the bound.
A program may use at most 128 MiB of HBM per device.

v0:
```python
import jax
import jax.numpy as jnp
from jax import lax
from jax.sharding import PartitionSpec as P


def from_behind(shard, axis, by):
    length = lax.axis_size(axis)
    pairs = [(i, i + by) for i in range(length) if 0 <= i + by < length]
    return lax.ppermute(shard, axis, pairs)


def route_tables(route_col, score_rows, experts, capacity):
    expert_ids = jnp.arange(experts, dtype=jnp.int32)
    onehot = (route_col[:, None] == expert_ids).astype(jnp.int32)
    earlier = jnp.cumsum(onehot, axis=0) - onehot
    slot = jnp.sum(onehot * earlier, axis=1)
    position = route_col * capacity + slot
    raised = jnp.exp(score_rows)
    weights = raised / jnp.sum(raised, axis=1, keepdims=True)
    gate = lax.optimization_barrier(weights[:, 0].astype(jnp.bfloat16)).astype(jnp.float32)
    table = position[:, None] == jnp.arange(experts * capacity, dtype=jnp.int32)
    return (weights, gate, table)


def per_device(inputs, routes, router_scores, cotangent, w_gate, w_up, w_down):
    tokens_in = inputs[0]
    upstream = cotangent[0]
    route_col = routes[0][:, 0]
    score_rows = router_scores[0]
    gate_mat = w_gate[0, 0]
    up_mat = w_up[0, 0]
    down_mat = w_down[0, 0]
    experts = lax.axis_size("expert")
    groups = lax.axis_size("dp")
    token_count, model_width = tokens_in.shape
    capacity = max(2, token_count * 5 // (4 * experts))
    weights, gate, table = route_tables(route_col, score_rows, experts, capacity)
    table_half = table.astype(jnp.bfloat16)
    token_contract = (((0,), (0,)), ((), ()))
    feature_contract = (((1,), (1,)), ((), ()))
    local_x = lax.dot_general(
        table_half, tokens_in, token_contract, preferred_element_type=jnp.float32
    )
    local_x = local_x.astype(jnp.bfloat16).reshape(experts, capacity, model_width)
    local_upstream = lax.dot_general(
        table_half, upstream, token_contract, preferred_element_type=jnp.float32
    )
    local_upstream = local_upstream.astype(jnp.bfloat16).reshape(experts, capacity, model_width)
    local_gate = jnp.sum(jnp.where(table, gate[:, None], jnp.float32(0.0)), axis=0)
    local_gate = local_gate.astype(jnp.bfloat16).reshape(experts, capacity)
    copies_x = jnp.broadcast_to(local_x[:, None], (experts, groups, capacity, model_width)).reshape(
        experts * groups, capacity, model_width
    )
    copies_upstream = jnp.broadcast_to(
        local_upstream[:, None], (experts, groups, capacity, model_width)
    ).reshape(experts * groups, capacity, model_width)
    copies_gate = jnp.broadcast_to(local_gate[:, None], (experts, groups, capacity)).reshape(
        experts * groups, capacity
    )
    rows_x, rows_upstream, rows_gate = (
        lax.all_to_all(copies_x, ("expert", "dp"), split_axis=0, concat_axis=0, tiled=True),
        lax.all_to_all(copies_upstream, ("expert", "dp"), split_axis=0, concat_axis=0, tiled=True),
        lax.all_to_all(copies_gate, ("expert", "dp"), split_axis=0, concat_axis=0, tiled=True),
    )
    rows_x = rows_x.reshape(-1, model_width)
    grid_upstream = rows_upstream.reshape(experts, groups, capacity, model_width)
    rows_grad = (
        rows_gate.reshape(-1).astype(jnp.float32)[:, None]
        * grid_upstream.reshape(-1, model_width).astype(jnp.float32)
    ).astype(jnp.bfloat16)
    gate_pre = lax.dot_general(
        rows_x, gate_mat, feature_contract, preferred_element_type=jnp.float32
    )
    up_pre = lax.dot_general(rows_x, up_mat, feature_contract, preferred_element_type=jnp.float32)
    gate_sig = jax.nn.sigmoid(gate_pre)
    activated = (gate_pre * gate_sig * up_pre).astype(jnp.bfloat16)
    partial_out = jnp.dot(activated, down_mat, preferred_element_type=jnp.float32)
    summed_out = lax.psum_scatter(
        partial_out.reshape(experts, groups, capacity, model_width).astype(jnp.bfloat16),
        "dp",
        scatter_dimension=1,
        tiled=True,
    )
    flat_out = lax.all_to_all(
        summed_out.reshape(experts, capacity, model_width),
        "expert",
        split_axis=0,
        concat_axis=0,
        tiled=True,
    ).reshape(-1, model_width)
    scores_grad = lax.dot_general(
        upstream, flat_out, feature_contract, preferred_element_type=jnp.float32
    )
    gate_grad = jnp.sum(jnp.where(table, scores_grad, jnp.float32(0.0)), axis=1)
    is_first = (jnp.arange(score_rows.shape[1]) == 0).astype(jnp.float32)
    score_grad = gate_grad[:, None] * weights[:, 0:1] * (is_first - weights)
    hidden_grad = lax.dot_general(
        rows_grad, down_mat, feature_contract, preferred_element_type=jnp.float32
    )
    pre_gate = (hidden_grad * up_pre * gate_sig * (1.0 + gate_pre * (1.0 - gate_sig))).astype(
        jnp.bfloat16
    )
    pre_up = (hidden_grad * gate_pre * gate_sig).astype(jnp.bfloat16)
    grad_down = lax.dot_general(
        activated, rows_grad, token_contract, preferred_element_type=jnp.float32
    ).astype(jnp.bfloat16)
    grad_gate = lax.dot_general(
        pre_gate, rows_x, token_contract, preferred_element_type=jnp.float32
    ).astype(jnp.bfloat16)
    grad_up = lax.dot_general(
        pre_up, rows_x, token_contract, preferred_element_type=jnp.float32
    ).astype(jnp.bfloat16)
    partial_in = jnp.dot(pre_gate, gate_mat, preferred_element_type=jnp.float32)
    partial_in = partial_in + jnp.dot(pre_up, up_mat, preferred_element_type=jnp.float32)
    outgoing = partial_in.astype(jnp.bfloat16).reshape(experts * groups, capacity, model_width)
    arrived = lax.all_to_all(outgoing, ("expert", "dp"), split_axis=0, concat_axis=0, tiled=True)
    flat_in = jnp.sum(
        arrived.reshape(experts, groups, capacity, model_width).astype(jnp.float32), axis=1
    )
    flat_in = flat_in.astype(jnp.bfloat16).reshape(-1, model_width)
    input_grad = jnp.dot(table_half, flat_in, preferred_element_type=jnp.float32).astype(
        jnp.bfloat16
    )
    handed = from_behind(input_grad, "pipe", -1)
    return (
        score_grad[None],
        handed[None],
        grad_gate[None, None],
        grad_up[None, None],
        grad_down[None, None],
    )


def solution(mesh):
    in_specs = (
        P("pipe", ("expert", "dp"), None),
        P("pipe", ("expert", "dp"), None),
        P("pipe", ("expert", "dp"), None),
        P("pipe", ("expert", "dp"), None),
        P("pipe", "expert", "dp", None),
        P("pipe", "expert", "dp", None),
        P("pipe", "expert", "dp", None),
    )
    out_specs = (
        P("pipe", ("expert", "dp"), None),
        P("pipe", ("expert", "dp"), None),
        P("pipe", "expert", "dp", None),
        P("pipe", "expert", "dp", None),
        P("pipe", "expert", "dp", None),
    )
    return jax.shard_map(
        per_device, mesh=mesh, in_specs=in_specs, out_specs=out_specs, check_vma=False
    )
```

profile of v0, /device:TPU:1, one launch (start us, length us, event | category | flops | bytes accessed | tf_op | source)
XLA Modules:
  0.0 615.7 jit_solution(7915761490829794387)
XLA Ops:
  11.9 6.4 %all-to-all-start.2 = ((bf16[8,1,80]{2,1,0:T(2,128)(2,1)}), bf16[8,1,80]{2,1,0:T(2,128)(2,1)S(1)}, u32[]{:S(2)}, u32[]{:S(2)}) async-start(bf16[8,1,80]{2,1,0:T(2,128)(2,1)} %copy.16), calls=%async_computation.2 | async-start | bytes 8192 | tf_op jit(solution)/shard_map/all_to_all | solution.py:64
  18.3 1.7 convolution_convert_fusion.5
  20.1 3.5 all-to-all-done.2
  23.6 3.0 broadcast_in_dim.57
  26.5 4.7 all-to-all-start
  31.2 1.7 convolution_convert_fusion.4
  32.9 112.7 %all-to-all-done = bf16[8,80,4096]{2,1,0:T(8,128)(2,1)} async-done(((bf16[8,80,4096]{2,1,0:T(8,128)(2,1)}), bf16[8,80,4096]{2,1,0:T(8,128)(2,1)}, u32[]{:S(2)}, u32[]{:S(2)}) %all-to-all-start) | async-done | bytes 5242912 | tf_op jit(solution)/shard_map/all_to_all | solution.py:62
  145.7 3.0 broadcast_in_dim.63
  148.6 4.8 all-to-all-start.3
  153.5 5.2 fusion.8
  158.7 5.2 fusion.12
  163.9 103.1 %all-to-all-done.3 = bf16[8,80,4096]{2,1,0:T(8,128)(2,1)} async-done(((bf16[8,80,4096]{2,1,0:T(8,128)(2,1)}), bf16[8,80,4096]{2,1,0:T(8,128)(2,1)}, u32[]{:S(2)}, u32[]{:S(2)}) %all-to-all-start.3) | async-done | bytes 5242912 | tf_op jit(solution)/shard_map/all_to_all | solution.py:63
  267.0 4.5 multiply_convert_fusion
  271.5 2.1 multiply_convert_fusion.1
  273.6 1.6 fusion.10
  275.2 3.9 add_convert_fusion
  279.1 5.1 all-to-all-start.4
  284.5 3.9 convolution_convert_fusion
  289.1 5.0 fusion.2
  294.1 5.0 fusion.1
  299.2 7.1 %fusion = bf16[640,4096]{1,0:T(8,128)(2,1)} fusion(f32[640]{0:T(1024)S(1)} %reshape.112, bf16[8,80,4096]{2,1,0:T(8,128)(2,1)} %all-to-all-done.3), kind=kLoop, calls=%fused_computation.1 | loop fusion | flops 7864320 | bytes 10488320 | tf_op jit(solution)/shard_map/convert_element_type | solution.py:71
  306.3 270.8 %all-reduce.3.cloned.1.call-done = bf16[2,4,80,4096]{3,2,1,0:T(8,128)(2,1)} async-done(((bf16[2,4,80,4096]{3,2,1,0:T(8,128)(2,1)}), bf16[2,4,80,4096]{3,2,1,0:T(8,128)(2,1)}) %all-reduce.3.cloned.1.call-update) | async-done | bytes 5242896
  577.1 3.1 dynamic-slice_bitcast_fusion
  580.3 4.7 all-to-all-start.1
  585.0 3.6 bitcast_reduce_fusion
  588.6 1.5 convolution_convert_fusion.6
  590.0 2.7 collective-permute-start
  592.8 2.5 fusion.3
  595.3 5.5 all-to-all-done.1
  600.9 2.1 fusion.15
  603.7 2.9 collective-permute-done
  606.6 2.3 copy.22
  (46 shorter events, 6.4 us)
Async XLA Ops:
  7.2 264.3 %copy-start = (bf16[1,1,192,4096]{3,2,1,0:T(8,128)(2,1)S(1)}, bf16[1,1,192,4096]{3,2,1,0:T(8,128)(2,1)}, u32[]{:S(2)}) copy-start(bf16[1,1,192,4096]{3,2,1,0:T(8,128)(2,1)} %param.13) | copy-start | bytes 4718596
  11.9 11.6 %all-to-all-start.2 = ((bf16[8,1,80]{2,1,0:T(2,128)(2,1)}), bf16[8,1,80]{2,1,0:T(2,128)(2,1)S(1)}, u32[]{:S(2)}, u32[]{:S(2)}) async-start(bf16[8,1,80]{2,1,0:T(2,128)(2,1)} %copy.16), calls=%async_computation.2 | async-start | bytes 8192 | tf_op jit(solution)/shard_map/all_to_all | solution.py:64
  26.5 119.1 %all-to-all-start = ((bf16[8,80,4096]{2,1,0:T(8,128)(2,1)}), bf16[8,80,4096]{2,1,0:T(8,128)(2,1)}, u32[]{:S(2)}, u32[]{:S(2)}) async-start(bf16[8,80,4096]{2,1,0:T(8,128)(2,1)} %bitcast.99), calls=%async_computation | async-start | bytes 10485760 | tf_op jit(solution)/shard_map/all_to_all | solution.py:62
  148.6 4.9 copy-start.3
  148.6 118.4 %all-to-all-start.3 = ((bf16[8,80,4096]{2,1,0:T(8,128)(2,1)}), bf16[8,80,4096]{2,1,0:T(8,128)(2,1)}, u32[]{:S(2)}, u32[]{:S(2)}) async-start(bf16[8,80,4096]{2,1,0:T(8,128)(2,1)} %bitcast.98), calls=%async_computation.3 | async-start | bytes 10485760 | tf_op jit(solution)/shard_map/all_to_all | solution.py:63
  153.4 5.3 copy-start.1
  267.0 4.5 copy-start.7
  267.0 4.5 copy-start.8
  271.5 2.1 copy-start.2
  273.6 1.6 copy-start.4
  279.1 301.1 %all-to-all-start.4 = ((bf16[8,80,4096]{2,1,0:T(8,128)(2,1)}), bf16[8,80,4096]{2,1,0:T(8,128)(2,1)}, u32[]{:S(2)}, u32[]{:S(2)}) async-start(bf16[8,80,4096]{2,1,0:T(8,128)(2,1)} %bitcast.97), calls=%async_computation.4 | async-start | bytes 10485760 | tf_op jit(solution)/shard_map/all_to_all | solution.py:117
  284.2 292.9 %all-reduce.3.cloned.1.call-start = ((), (), s32[]{:S(2)}) async-start(), calls=%async_computation.5 | async-start | bytes 10485760
  284.4 4.0 copy-start.6
  580.3 12.5 %slice-start = ((s8[5242880]{0:T(1024)(128)(4,1)}), s8[1048576]{0:T(1024)(128)(4,1)S(1)}, s32[]{:S(2)}) async-start(s8[5242880]{0:T(1024)(128)(4,1)} %bitcast.95), calls=%async_computation.6 | async-start | bytes 2097152
  580.3 20.6 %all-to-all-start.1 = ((bf16[2,80,4096]{2,1,0:T(8,128)(2,1)}), bf16[2,80,4096]{2,1,0:T(8,128)(2,1)}, u32[]{:S(2)}, u32[]{:S(2)}) async-start(bf16[2,80,4096]{2,1,0:T(8,128)(2,1)} %dynamic-slice_bitcast_fusion), calls=%async_computation.1 | async-start | bytes 2621440 | tf_op jit(solution)/shard_map/all_to_all | solution.py:85
  585.0 7.8 %slice-start.1 = ((s8[5242880]{0:T(1024)(128)(4,1)}), s8[4194304]{0:T(1024)(128)(4,1)S(1)}, s32[]{:S(2)}) async-start(s8[5242880]{0:T(1024)(128)(4,1)} %bitcast.95), calls=%async_computation.7 | async-start | bytes 8388608
  590.0 13.0 %copy-start.5 = (f32[1,128,8]{1,2,0:T(8,128)S(1)}, f32[1,128,8]{1,2,0:T(8,128)}, u32[]{:S(2)}) copy-start(f32[1,128,8]{1,2,0:T(8,128)} %param.9) | copy-start | bytes 12292
  590.0 16.6 %collective-permute-start = (bf16[128,4096]{1,0:T(8,128)(2,1)}, bf16[128,4096]{1,0:T(8,128)(2,1)}, u32[]{:S(2)}, u32[]{:S(2)}) collective-permute-start(bf16[128,4096]{1,0:T(8,128)(2,1)} %convolution_convert_fusion.6), channel_id=1, source_target_pairs={{8,0},{16,8},{24,16},{9,1},{17,9},{25,17},{10,2},{18,10},{26,18},{... | collective-permute-start | bytes 3145736 | tf_op jit(solution)/shard_map/ppermute | solution.py:10
Sparse Core Ops, SparseCore 0:
  288.5 288.5 all-reduce.2
where the time goes:
time: 617 us; the launch traced here: 616 us
  waiting for transfers between devices  499 us (81%)
  matrix products  41.6 us (7%)
  starting transfers between devices  28.4 us (5%)
  other arithmetic  19.9 us (3%)
  between operations  14.3 us (2%)
  local copies, waits for them, and re-layouts  12.9 us (2%)
    unnamed x2, waiting for transfers between devices  271 us
    all_to_all x1, waiting for transfers between devices, per_device(): lax.all_to_all(copies_x, ('expert', 'dp'), split_axis=0, concat_axis=0, t...  113 us
    all_to_all x1, waiting for transfers between devices, per_device(): lax.all_to_all(copies_upstream, ('expert', 'dp'), split_axis=0, concat_ax...  103 us
  transfers between devices with their start and end apart: 7, of which 6 were waited for; matrix products, arithmetic and copies ran while one was open for 8% of the time, Pallas kernels for 0%

commit v1 on v0

v1 whole, which is shorter than its diff:
```python
import functools

import jax
import jax.numpy as jnp
from jax import lax
from jax.experimental import pallas as pl
from jax.experimental.pallas import tpu as pltpu
from jax.sharding import PartitionSpec as P

MESH = pl.DeviceIdType.MESH
NT = (((1,), (1,)), ((), ()))
TN = (((0,), (0,)), ((), ()))


def compute_order(k, n):
    order = [k]
    for d in range(1, n):
        order += [b for b in (k - d, k + d) if 0 <= b < n]
    if n > 2 and k in (0, n - 1):
        order = [k] + order[2:] + [order[1]]
    if k >= n // 2 and 0 < k < n - 1:
        order = [k]
        for d in range(1, n):
            order += [b for b in (k + d, k - d) if 0 <= b < n]
    return order


def finish_order(k, n):
    if k in (0, n - 1):
        return []
    rightward = list(range(k + 1, n))
    leftward = list(range(k - 1, -1, -1))
    return rightward + leftward if k < n // 2 else leftward + rightward


def kernel(
    dims, x_ref, up_ref, gate_ref, tab_ref, nxt_ref, wg_ref, wu_ref, wd_ref,
    out_ref, gg_ref, gu_ref, gd_ref, s_ref,
    stage, xb, yb, dxb, dxr, hrecv, act, pg, pu, sbuf, srecv,
    ey_send, ey_recv, f_send, f_recv, r_send, r_recv, s_send, s_recv, h_send, h_recv,
):
    pipes, experts, n, cap, depth = dims
    rows = experts * cap
    p, y, z = lax.axis_index("pipe"), lax.axis_index("expert"), lax.axis_index("dp")
    tokens, width = x_ref.shape

    def peer(de, dz):
        return lax.rem(y + de, experts), lax.rem(z + dz, n)

    others = [(de, dz) for de in range(experts) for dz in range(n) if (de, dz) != (0, 0)]

    barrier = pltpu.get_barrier_semaphore()
    for de, dz in others:
        ey, ez = peer(de, dz)
        pl.semaphore_signal(barrier, inc=1, device_id=(p, ey, ez), device_id_type=MESH)

    @pl.when(p > 0)
    def _():
        for e in range(experts):
            pl.semaphore_signal(barrier, inc=1, device_id=(p - 1, e, z), device_id_type=MESH)

    @pl.when(p < pipes - 1)
    def _():
        for e in range(experts):
            pl.semaphore_signal(barrier, inc=1, device_id=(p + 1, e, z), device_id_type=MESH)

    def block(ref, b):
        return ref.at[pl.ds(b * rows, rows)]

    tab = tab_ref[...]
    step = min(512, width)

    def pack(t, buffer):
        def tile(j, c):
            cols = pl.ds(pl.multiple_of(j * step, step), step)
            if t == 0:
                vals = x_ref[:, cols]
            else:
                vals = (gate_ref[...] * up_ref[:, cols].astype(jnp.float32)).astype(jnp.bfloat16)
            stage[t, :, cols] = jnp.dot(tab, vals, preferred_element_type=jnp.float32).astype(jnp.bfloat16)
            return c

        lax.fori_loop(0, width // step, tile, 0)

    def exchange(t, buffer, de):
        e = lax.rem(y + de, experts)
        return pltpu.make_async_remote_copy(
            src_ref=stage.at[t, pl.ds(pl.multiple_of(e * cap, 16), cap)],
            dst_ref=buffer.at[pl.ds(pl.multiple_of(z * rows + y * cap, 16), cap)],
            send_sem=ey_send.at[t, de], recv_sem=ey_recv.at[t, de],
            device_id=(p, e, z), device_id_type=MESH,
        )

    pack(0, xb)
    around = (p > 0).astype(jnp.int32) + (p < pipes - 1).astype(jnp.int32)
    pl.semaphore_wait(barrier, len(others) + experts * around)

    for t, buffer in ((0, xb), (1, yb)):
        if t:
            pack(1, yb)
        for de in range(1, experts):
            exchange(t, buffer, de).start()
        own = pl.ds(pl.multiple_of(z * rows + y * cap, 16), cap)
        buffer[own] = stage[t, pl.ds(pl.multiple_of(y * cap, 16), cap)]

    def forward(b, t, side):
        buffer = (xb, yb)[t]
        return pltpu.make_async_remote_copy(
            src_ref=block(buffer, b), dst_ref=block(buffer, b),
            send_sem=f_send.at[side, b, t], recv_sem=f_recv.at[side, b, t],
            device_id=(p, y, z + (1 if side else -1)), device_id_type=MESH,
        )

    def running(k, b, side):
        slot = n if (not side and b == k - 1) else b
        return pltpu.make_async_remote_copy(
            src_ref=block(dxb, b), dst_ref=block(dxr, slot),
            send_sem=r_send.at[b], recv_sem=r_recv.at[slot],
            device_id=(p, y, z + (1 if side else -1)), device_id_type=MESH,
        )

    def taken(slot):
        pltpu.make_async_copy(block(dxr, slot), block(dxr, slot), r_recv.at[slot]).wait()

    def arrive(k, b, t):
        side = 1 if b < k else 0
        forward(b, t, side).wait_recv()
        if side and k < n - 1 or not side and k > 0:
            forward(b, t, side).start()

    def near_end(k, side):
        return n > 2 and (side and k == n - 2 or not side and k == 1)

    def sides(k):
        return ([1] if k < n - 1 else []) + ([0] if k > 0 else [])

    for t, buffer in ((0, xb), (1, yb)):
        for de in range(1, experts):
            exchange(t, buffer, de).wait_recv()
        for k in range(n):
            @pl.when(z == k)
            def _():
                for side in sides(k):
                    if t == 0 or not near_end(k, side):
                        forward(k, t, side).start()

    def work(b):
        off = pl.multiple_of(b * rows, 16)
        here = pl.ds(off, rows)
        deep = min(1024, width)

        def into(j, c):
            cols = pl.ds(pl.multiple_of(j * deep, deep), deep)
            xt, yt = xb[here, cols], yb[here, cols]
            g, u, a = c
            g = g + lax.dot_general(xt, wg_ref[:, cols], NT, preferred_element_type=jnp.float32)
            u = u + lax.dot_general(xt, wu_ref[:, cols], NT, preferred_element_type=jnp.float32)
            a = a + lax.dot_general(yt, wd_ref[:, cols], NT, preferred_element_type=jnp.float32)
            return g, u, a

        zero = jnp.zeros((rows, depth), jnp.float32)
        g, u, a = lax.fori_loop(0, width // deep, into, (zero, zero, zero))
        sig = 1.0 / (1.0 + jnp.exp(-g))
        silu = g * sig
        hidden = (silu * u).astype(jnp.bfloat16)
        act[here] = hidden
        total = jnp.sum(hidden.astype(jnp.float32) * a, axis=1, keepdims=True)
        sbuf[here] = jnp.broadcast_to(total, (rows, 128))
        dg = (a * u * sig * (1.0 + g * (1.0 - sig))).astype(jnp.bfloat16)
        du = (a * silu).astype(jnp.bfloat16)
        pg[here] = dg
        pu[here] = du

        def back(j, c):
            cols = pl.ds(pl.multiple_of(j * step, step), step)
            part = jnp.dot(pg[here], wg_ref[:, cols], preferred_element_type=jnp.float32)
            part = part + jnp.dot(pu[here], wu_ref[:, cols], preferred_element_type=jnp.float32)
            dxb[here, cols] = part.astype(jnp.bfloat16)
            return c

        lax.fori_loop(0, width // step, back, 0)

    orders = [compute_order(k, n) for k in range(n)]
    for i in range(n):
        if i:
            for k in range(n):
                @pl.when(z == k)
                def _():
                    b = orders[k][i]
                    if n > 2 and k in (0, n - 1):
                        if i == 1:
                            arrive(k, orders[k][n - 1], 0)
                        for t in range(2):
                            if t or i < n - 1:
                                arrive(k, b, t)
                    else:
                        d = abs(b - k)
                        pair = [c for c in (k - d, k + d) if 0 <= c < n]
                        if all(orders[k].index(c) >= i for c in pair):
                            for t in range(2):
                                for c in pair:
                                    arrive(k, c, t)
                        if i == n - 1:
                            for side in sides(k):
                                if near_end(k, side):
                                    forward(k, 1, side).start()
        b = 0
        for k in range(n):
            b = b + (z == k).astype(jnp.int32) * orders[k][i]
        work(b)
        if i:
            for k in (0, n - 1):
                @pl.when(z == k)
                def _():
                    running(k, orders[k][i], 0 if k else 1).start()

    def tell(de, dz):
        ey, ez = peer(de, dz)
        return pltpu.make_async_remote_copy(
            src_ref=sbuf.at[pl.ds(pl.multiple_of(ez * rows + ey * cap, 16), cap)],
            dst_ref=srecv.at[z, pl.ds(pl.multiple_of(y * cap, 16), cap)],
            send_sem=s_send.at[de, dz], recv_sem=s_recv.at[de, dz],
            device_id=(p, ey, ez), device_id_type=MESH,
        )

    for de, dz in others:
        tell(de, dz).start()
    srecv[z, pl.ds(pl.multiple_of(y * cap, 16), cap)] = sbuf[
        pl.ds(pl.multiple_of(z * rows + y * cap, 16), cap)
    ]

    def weights(j, c):
        cols = pl.ds(pl.multiple_of(j * step, step), step)
        yt, xt = yb[:, cols], xb[:, cols]
        gd_ref[:, cols] = lax.dot_general(act[...], yt, TN, preferred_element_type=jnp.float32).astype(jnp.bfloat16)
        gg_ref[:, cols] = lax.dot_general(pg[...], xt, TN, preferred_element_type=jnp.float32).astype(jnp.bfloat16)
        gu_ref[:, cols] = lax.dot_general(pu[...], xt, TN, preferred_element_type=jnp.float32).astype(jnp.bfloat16)
        return c

    lax.fori_loop(0, width // step, weights, 0)

    def add(b, slots):
        def some(j, c):
            here = pl.ds(pl.multiple_of(b * rows + j * 16, 16), 16)
            total = dxb[here].astype(jnp.float32)
            for slot in slots:
                total = total + dxr[pl.ds(pl.multiple_of(slot * rows + j * 16, 16), 16)].astype(jnp.float32)
            dxb[here] = total.astype(jnp.bfloat16)
            return c

        lax.fori_loop(0, rows // 16, some, 0)

    for k in range(n):
        @pl.when(z == k)
        def _():
            for b in finish_order(k, n):
                side = 1 if b > k else 0
                taken(b)
                add(b, [b])
                running(k, b, side).start()
            slots = ([k] if k > 0 else []) + ([n] if k < n - 1 else [])
            for slot in slots:
                taken(slot)
            add(k, slots)

    def hand(e):
        return pltpu.make_async_remote_copy(
            src_ref=dxb.at[pl.ds(pl.multiple_of(z * rows + e * cap, 16), cap)],
            dst_ref=hrecv.at[pl.ds(pl.multiple_of(y * cap, 16), cap)],
            send_sem=h_send.at[e], recv_sem=h_recv.at[y],
            device_id=(p - 1, e, z), device_id_type=MESH,
        )

    @pl.when(p > 0)
    def _():
        for e in range(experts):
            hand(e).start()

    for de, dz in others:
        tell(de, dz).wait_recv()
    total = srecv[0]
    for k in range(1, n):
        total = total + srecv[k]
    s_ref[...] = total

    @pl.when(p < pipes - 1)
    def _():
        for e in range(experts):
            pltpu.make_async_copy(hrecv.at[pl.ds(e * cap, cap)], hrecv.at[pl.ds(e * cap, cap)], h_recv.at[e]).wait()

        def tile(j, c):
            cols = pl.ds(pl.multiple_of(j * step, step), step)
            out_ref[:, cols] = lax.dot_general(
                nxt_ref[...], hrecv[:, cols], TN, preferred_element_type=jnp.float32
            ).astype(jnp.bfloat16)
            return c

        lax.fori_loop(0, width // step, tile, 0)

    @pl.when(p == pipes - 1)
    def _():
        out_ref[...] = jnp.zeros_like(out_ref)

    for t, buffer in ((0, xb), (1, yb)):
        for de in range(1, experts):
            exchange(t, buffer, de).wait_send()
    for de, dz in others:
        tell(de, dz).wait_send()
    for k in range(n):
        @pl.when(z == k)
        def _():
            for b in range(n):
                for side in sides(k):
                    if b == k or (b < k and side) or (b > k and not side):
                        for t in range(2):
                            forward(b, t, side).wait_send()
                if b != k:
                    running(k, b, 1 if b > k else 0).wait_send()

    @pl.when(p > 0)
    def _():
        for e in range(experts):
            hand(e).wait_send()


def tables(route_col, experts, capacity, padded):
    expert_ids = jnp.arange(experts, dtype=jnp.int32)
    onehot = (route_col[:, None] == expert_ids).astype(jnp.int32)
    earlier = jnp.cumsum(onehot, axis=0) - onehot
    slot = jnp.sum(onehot * earlier, axis=1)
    position = route_col * padded + slot
    return (jnp.arange(experts * padded, dtype=jnp.int32)[:, None] == position[None, :])


def per_device(inputs, routes, router_scores, cotangent, w_gate, w_up, w_down):
    experts, n, pipes = lax.axis_size("expert"), lax.axis_size("dp"), lax.axis_size("pipe")
    tokens, width = inputs.shape[1:]
    depth = w_gate.shape[2]
    capacity = max(2, tokens * 5 // (4 * experts))
    cap = -(-capacity // 16) * 16
    rows = experts * cap
    route_col = routes[0, :, 0]
    behind = lax.ppermute(route_col, "pipe", [(i + 1, i) for i in range(pipes - 1)])
    table = tables(route_col, experts, capacity, cap)
    following = tables(behind, experts, capacity, cap).astype(jnp.bfloat16)
    raised = jnp.exp(router_scores[0])
    weights = raised / jnp.sum(raised, axis=1, keepdims=True)
    gate = lax.optimization_barrier(weights[:, 0:1].astype(jnp.bfloat16)).astype(jnp.float32)

    vmem = pl.BlockSpec(memory_space=pltpu.VMEM)
    half, full = jnp.bfloat16, jnp.float32
    dma = pltpu.SemaphoreType.DMA
    grad = jax.ShapeDtypeStruct((depth, width), half)
    handed, grad_gate, grad_up, grad_down, sums = pl.pallas_call(
        functools.partial(kernel, (pipes, experts, n, cap, depth)),
        out_shape=(
            jax.ShapeDtypeStruct((tokens, width), half), grad, grad, grad,
            jax.ShapeDtypeStruct((rows, 128), full),
        ),
        in_specs=[vmem] * 8,
        out_specs=(vmem,) * 5,
        scratch_shapes=[
            pltpu.VMEM((2, rows, width), half),
            pltpu.VMEM((n * rows, width), half),
            pltpu.VMEM((n * rows, width), half),
            pltpu.VMEM((n * rows, width), half),
            pltpu.VMEM(((n + 1) * rows, width), half),
            pltpu.VMEM((rows, width), half),
            pltpu.VMEM((n * rows, depth), half),
            pltpu.VMEM((n * rows, depth), half),
            pltpu.VMEM((n * rows, depth), half),
            pltpu.VMEM((n * rows, 128), full),
            pltpu.VMEM((n, rows, 128), full),
            dma((2, experts)), dma((2, experts)),
            dma((2, n, 2)), dma((2, n, 2)),
            dma((n,)), dma((n + 1,)),
            dma((experts, n)), dma((experts, n)),
            dma((experts,)), dma((experts,)),
        ],
        compiler_params=pltpu.CompilerParams(
            collective_id=0, has_side_effects=True, vmem_limit_bytes=62 * 1024 * 1024
        ),
    )(
        inputs[0], cotangent[0], gate, table.astype(half), following,
        w_gate[0, 0], w_up[0, 0], w_down[0, 0],
    )
    gate_grad = jnp.sum(jnp.where(table, sums[:, 0:1], 0.0), axis=0)[:, None] / gate
    is_first = (jnp.arange(router_scores.shape[2]) == 0).astype(full)
    score_grad = gate_grad * weights[:, 0:1] * (is_first - weights)
    return (
        score_grad[None],
        handed[None],
        grad_gate[None, None],
        grad_up[None, None],
        grad_down[None, None],
    )


def solution(mesh):
    rows = P("pipe", ("expert", "dp"), None)
    mats = P("pipe", "expert", "dp", None)
    return jax.shard_map(
        per_device, mesh=mesh, in_specs=(rows,) * 4 + (mats,) * 3,
        out_specs=(rows, rows, mats, mats, mats), check_vma=False,
    )
```

time: 617 us -> 296 us (0.48)
  waiting for transfers between devices: 499 us -> 0.01 us
  Pallas kernels: 0 us -> 275 us
  matrix products: 41.6 us -> 0 us
  starting transfers between devices: 28.4 us -> 1.97 us
  other arithmetic: 19.9 us -> 5.35 us
  between operations: 14.3 us -> 0.74 us
    pallas_call x0 -> x1, Pallas kernels: none -> 275 us  [per_device(): pl.pallas_call(functools.partial(kernel, (pipes, experts, n, cap, depth))...]
    unnamed x2 -> x0, waiting for transfers between devices: 271 us -> none
    all_to_all x5 -> x0, waiting for transfers between devices: 225 us -> none  [the longest x1 113 us: per_device(): lax.all_to_all(copies_x, ('expert', 'dp'), split_axis=0, concat_axis=0, t...]
    dot_general x13 -> x0, matrix products: 41.6 us -> none  [the longest x1 5.25 us: per_device(): lax.dot_general(rows_x, up_mat, feature_contract, preferred_element_type=...]
    all_to_all x5 -> x0, starting transfers between devices: 25.6 us -> none  [the longest x1 6.38 us: per_device(): lax.all_to_all(copies_gate, ('expert', 'dp'), split_axis=0, concat_axis=0...]
    convert_element_type x7, other arithmetic: 12.4 us -> 2.83 us  [the longest x2 0.82 us: tables(): onehot = (route_col[:, None] == expert_ids).astype(jnp.int32)]
  transfers between devices with their start and end apart: 7 -> 1, of which waited for: 6 -> 0; matrix products, arithmetic and copies ran while one was open for 8% -> 2% of each run, Pallas kernels for 0% -> 0%
where the time goes in v1:
time: 296 us; the launch traced here: 293 us
  Pallas kernels  275 us (93%)
  local copies, waits for them, and re-layouts  10.1 us (3%)
  other arithmetic  5.35 us (2%)
    pallas_call x1, Pallas kernels, per_device(): pl.pallas_call(functools.partial(kernel, (pipes, experts, n, cap, depth))...  275 us
    unnamed x12, local copies, waits for them, and re-layouts  8.83 us
  transfers between devices with their start and end apart: 1, of which 0 were waited for; matrix products, arithmetic and copies ran while one was open for 2% of the time, Pallas kernels for 0%

profile of v1, /device:TPU:1, one launch (start us, length us, event | category | flops | bytes accessed | tf_op | source)
XLA Modules:
  0.0 292.9 jit_solution(13833631343581954744)
XLA Ops:
  0.6 2.0 collective-permute-start
  2.6 0.7 fusion.3
  3.4 0.8 copy.15
  4.1 0.2 reduce_window_sum.17
  4.3 0.8 select_reduce_fusion.2
  5.1 0.7 multiply_add_fusion.1
  5.8 0.6 fusion.tab_ref
  6.4 0.1 exponential_bitcast_fusion
  6.6 0.1 fusion.4
  6.7 0.6 convert_element_type.27.gate_ref
  7.3 0.0 collective-permute-done
  7.3 0.1 fusion.2
  7.4 0.2 reduce_window_sum.18
  7.6 0.2 select_reduce_fusion.1
  7.8 0.6 fusion.1.nxt_ref
  8.4 274.8 %shard_map.110 = (bf16[128,4096]{1,0:T(8,128)(2,1)}, bf16[192,4096]{1,0:T(8,128)(2,1)}, bf16[192,4096]{1,0:T(8,128)(2,1)}, bf16[192,4096]{1,0:T(8,128)(2,1)}, f32[160,128]{1,0:T(8,128)}) custom-call(bf16[128,4096]{1,0:T(8,128)(2,1)} %bitcast.21, bf16[128,4096]{1,0:T(8,128)(2,1)} %bitcast.22, f32[128,1]{1,0:T(8,128)} %convert_element_type.27.gate_ref, ...), custom_call_target="tpu_custom_call" | custom-call | tf_op jit(solution)/shard_map/pallas_call | solution.py:354
  283.2 0.0 copy-start.2
  283.2 1.1 slice_reduce_fusion
  284.4 0.1 select_reduce_fusion
  284.5 0.1 copy.16
  284.6 0.2 multiply_reduce_fusion
  284.8 0.1 subtract_multiply_fusion
  284.9 0.7 copy.17
  285.5 2.3 copy.22
  287.8 0.0 copy-done.2
  287.8 0.0 copy-start.1
  287.8 1.1 copy.23
  289.0 0.8 copy-done.1
  289.8 0.0 copy-start
  289.8 1.1 copy.24
  291.0 0.8 copy-done
  291.8 1.1 copy.25
  (2 shorter events, 0.0 us)
Async XLA Ops:
  0.6 6.7 %collective-permute-start = (s32[128]{0:T(128)}, s32[128]{0:T(128)S(1)}, u32[]{:S(2)}, u32[]{:S(2)}) collective-permute-start(s32[128]{0:T(128)} %bitcast.23), channel_id=1, source_target_pairs={{8,0},{16,8},{24,16},{9,1},{17,9},{25,17},{10,2},{18,10},{26,18},{... | collective-permute-start | bytes 1544 | tf_op jit(solution)/shard_map/ppermute | solution.py:343
  283.2 4.6 %copy-start.2 = (bf16[192,4096]{1,0:T(8,128)(2,1)S(1)}, bf16[192,4096]{1,0:T(8,128)(2,1)}, u32[]{:S(2)}) copy-start(bf16[192,4096]{1,0:T(8,128)(2,1)} %get-tuple-element.12) | copy-start | bytes 4718596
  287.8 2.0 copy-start.1
  289.8 2.0 copy-start

commit v2 on v1

--- a/solution.py
+++ b/solution.py
@@ -64,8 +64,10 @@
         for e in range(experts):
             pl.semaphore_signal(barrier, inc=1, device_id=(p + 1, e, z), device_id_type=MESH)
 
-    def block(ref, b):
-        return ref.at[pl.ds(b * rows, rows)]
+    begin, length = (0, cap), (cap, rows - cap)
+
+    def piece(ref, b, q):
+        return ref.at[pl.ds(pl.multiple_of(b * rows + begin[q], 16), length[q])]
 
     tab = tab_ref[...]
     step = min(512, width)
@@ -86,7 +88,7 @@
         e = lax.rem(y + de, experts)
         return pltpu.make_async_remote_copy(
             src_ref=stage.at[t, pl.ds(pl.multiple_of(e * cap, 16), cap)],
-            dst_ref=buffer.at[pl.ds(pl.multiple_of(z * rows + y * cap, 16), cap)],
+            dst_ref=buffer.at[pl.ds(pl.multiple_of(z * rows + (experts - de) * cap, 16), cap)],
             send_sem=ey_send.at[t, de], recv_sem=ey_recv.at[t, de],
             device_id=(p, e, z), device_id_type=MESH,
         )
@@ -94,59 +96,62 @@
     pack(0, xb)
     around = (p > 0).astype(jnp.int32) + (p < pipes - 1).astype(jnp.int32)
     pl.semaphore_wait(barrier, len(others) + experts * around)
+
+    def forward(b, t, q, side):
+        buffer = (xb, yb)[t]
+        return pltpu.make_async_remote_copy(
+            src_ref=piece(buffer, b, q), dst_ref=piece(buffer, b, q),
+            send_sem=f_send.at[side, b, t, q], recv_sem=f_recv.at[side, b, t, q],
+            device_id=(p, y, z + (1 if side else -1)), device_id_type=MESH,
+        )
+
+    def running(k, b, q, side):
+        slot = n if (not side and b == k - 1) else b
+        return pltpu.make_async_remote_copy(
+            src_ref=piece(dxb, b, q), dst_ref=piece(dxr, slot, q),
+            send_sem=r_send.at[b, q], recv_sem=r_recv.at[slot, q],
+            device_id=(p, y, z + (1 if side else -1)), device_id_type=MESH,
+        )
+
+    def taken(slot, q):
+        whole = piece(dxr, slot, q)
+        pltpu.make_async_copy(whole, whole, r_recv.at[slot, q]).wait()
+
+    def arrive(k, b, t, q):
+        side = 1 if b < k else 0
+        forward(b, t, q, side).wait_recv()
+        if side and k < n - 1 or not side and k > 0:
+            forward(b, t, q, side).start()
+
+    def near_end(k, side):
+        return n > 2 and (side and k == n - 2 or not side and k == 1)
+
+    def sides(k):
+        return ([1] if k < n - 1 else []) + ([0] if k > 0 else [])
+
+    def depart(t, q):
+        for k in range(n):
+            @pl.when(z == k)
+            def _():
+                for side in sides(k):
+                    if t == 0 or not near_end(k, side):
+                        forward(k, t, q, side).start()
 
     for t, buffer in ((0, xb), (1, yb)):
         if t:
             pack(1, yb)
         for de in range(1, experts):
             exchange(t, buffer, de).start()
-        own = pl.ds(pl.multiple_of(z * rows + y * cap, 16), cap)
-        buffer[own] = stage[t, pl.ds(pl.multiple_of(y * cap, 16), cap)]
-
-    def forward(b, t, side):
-        buffer = (xb, yb)[t]
-        return pltpu.make_async_remote_copy(
-            src_ref=block(buffer, b), dst_ref=block(buffer, b),
-            send_sem=f_send.at[side, b, t], recv_sem=f_recv.at[side, b, t],
-            device_id=(p, y, z + (1 if side else -1)), device_id_type=MESH,
-        )
-
-    def running(k, b, side):
-        slot = n if (not side and b == k - 1) else b
-        return pltpu.make_async_remote_copy(
-            src_ref=block(dxb, b), dst_ref=block(dxr, slot),
-            send_sem=r_send.at[b], recv_sem=r_recv.at[slot],
-            device_id=(p, y, z + (1 if side else -1)), device_id_type=MESH,
-        )
-
-    def taken(slot):
-        pltpu.make_async_copy(block(dxr, slot), block(dxr, slot), r_recv.at[slot]).wait()
-
-    def arrive(k, b, t):
-        side = 1 if b < k else 0
-        forward(b, t, side).wait_recv()
-        if side and k < n - 1 or not side and k > 0:
-            forward(b, t, side).start()
-
-    def near_end(k, side):
-        return n > 2 and (side and k == n - 2 or not side and k == 1)
-
-    def sides(k):
-        return ([1] if k < n - 1 else []) + ([0] if k > 0 else [])
-
+        buffer[pl.ds(pl.multiple_of(z * rows, 16), cap)] = stage[t, pl.ds(pl.multiple_of(y * cap, 16), cap)]
+        depart(t, 0)
     for t, buffer in ((0, xb), (1, yb)):
         for de in range(1, experts):
             exchange(t, buffer, de).wait_recv()
-        for k in range(n):
-            @pl.when(z == k)
-            def _():
-                for side in sides(k):
-                    if t == 0 or not near_end(k, side):
-                        forward(k, t, side).start()
-
-    def work(b):
-        off = pl.multiple_of(b * rows, 16)
-        here = pl.ds(off, rows)
+        depart(t, 1)
+
+    def work(b, start, size):
+        off = pl.multiple_of(b * rows + start, 16)
+        here = pl.ds(off, size)
         deep = min(1024, width)
 
         def into(j, c):
@@ -158,14 +163,14 @@
             a = a + lax.dot_general(yt, wd_ref[:, cols], NT, preferred_element_type=jnp.float32)
             return g, u, a
 
-        zero = jnp.zeros((rows, depth), jnp.float32)
+        zero = jnp.zeros((size, depth), jnp.float32)
         g, u, a = lax.fori_loop(0, width // deep, into, (zero, zero, zero))
         sig = 1.0 / (1.0 + jnp.exp(-g))
         silu = g * sig
         hidden = (silu * u).astype(jnp.bfloat16)
         act[here] = hidden
         total = jnp.sum(hidden.astype(jnp.float32) * a, axis=1, keepdims=True)
-        sbuf[here] = jnp.broadcast_to(total, (rows, 128))
+        sbuf[here] = jnp.broadcast_to(total, (size, 128))
         dg = (a * u * sig * (1.0 + g * (1.0 - sig))).astype(jnp.bfloat16)
         du = (a * silu).astype(jnp.bfloat16)
         pg[here] = dg
@@ -181,43 +186,54 @@
         lax.fori_loop(0, width // step, back, 0)
 
     orders = [compute_order(k, n) for k in range(n)]
+    both = ((0, 0), (1, 0), (0, 1), (1, 1))
     for i in range(n):
-        if i:
-            for k in range(n):
-                @pl.when(z == k)
-                def _():
-                    b = orders[k][i]
-                    if n > 2 and k in (0, n - 1):
-                        if i == 1:
-                            arrive(k, orders[k][n - 1], 0)
-                        for t in range(2):
-                            if t or i < n - 1:
-                                arrive(k, b, t)
-                    else:
-                        d = abs(b - k)
-                        pair = [c for c in (k - d, k + d) if 0 <= c < n]
-                        if all(orders[k].index(c) >= i for c in pair):
-                            for t in range(2):
-                                for c in pair:
-                                    arrive(k, c, t)
-                        if i == n - 1:
-                            for side in sides(k):
-                                if near_end(k, side):
-                                    forward(k, 1, side).start()
         b = 0
         for k in range(n):
             b = b + (z == k).astype(jnp.int32) * orders[k][i]
-        work(b)
-        if i:
-            for k in (0, n - 1):
+        last = n > 1 and i == n - 1
+        for part in ((0, 1) if last else (None,)):
+            items = [item for item in both if part is None or item[1] == part]
+            for k in range(n) if i else ():
                 @pl.when(z == k)
                 def _():
-                    running(k, orders[k][i], 0 if k else 1).start()
+                    c = orders[k][i]
+                    if k in (0, n - 1):
+                        for t, q in items:
+                            arrive(k, c, t, q)
+                    else:
+                        d = abs(c - k)
+                        pair = [e for e in (k - d, k + d) if 0 <= e < n]
+                        if last and len(pair) == 1 or not last and all(orders[k].index(e) >= i for e in pair):
+                            for t, q in items:
+                                for e in pair:
+                                    arrive(k, e, t, q)
+                        if last and part == 1:
+                            for side in sides(k):
+                                if near_end(k, side):
+                                    forward(k, 1, 0, side).start()
+            if part is None:
+                work(b, 0, rows)
+            else:
+                work(b, begin[part], length[part])
+            if last and part == 1:
+                for k in range(n):
+                    for side in sides(k):
+                        if near_end(k, side):
+                            @pl.when(z == k)
+                            def _():
+                                forward(k, 1, 1, side).start()
+            if i:
+                for k in (0, n - 1):
+                    @pl.when((z == k) & (p > 0))
+                    def _():
+                        for q in (0, 1) if part is None else (part,):
+                            running(k, orders[k][i], q, 0 if k else 1).start()
 
     def tell(de, dz):
         ey, ez = peer(de, dz)
         return pltpu.make_async_remote_copy(
-            src_ref=sbuf.at[pl.ds(pl.multiple_of(ez * rows + ey * cap, 16), cap)],
+            src_ref=sbuf.at[pl.ds(pl.multiple_of(ez * rows + de * cap, 16), cap)],
             dst_ref=srecv.at[z, pl.ds(pl.multiple_of(y * cap, 16), cap)],
             send_sem=s_send.at[de, dz], recv_sem=s_recv.at[de, dz],
             device_id=(p, ey, ez), device_id_type=MESH,
@@ -226,7 +242,7 @@
     for de, dz in others:
         tell(de, dz).start()
     srecv[z, pl.ds(pl.multiple_of(y * cap, 16), cap)] = sbuf[
-        pl.ds(pl.multiple_of(z * rows + y * cap, 16), cap)
+        pl.ds(pl.multiple_of(z * rows, 16), cap)
     ]
 
     def weights(j, c):
@@ -239,42 +255,41 @@
 
     lax.fori_loop(0, width // step, weights, 0)
 
-    def add(b, slots):
+    def add(b, slots, q):
         def some(j, c):
-            here = pl.ds(pl.multiple_of(b * rows + j * 16, 16), 16)
+            here = pl.ds(pl.multiple_of(b * rows + begin[q] + j * 16, 16), 16)
             total = dxb[here].astype(jnp.float32)
             for slot in slots:
-                total = total + dxr[pl.ds(pl.multiple_of(slot * rows + j * 16, 16), 16)].astype(jnp.float32)
+                there = pl.ds(pl.multiple_of(slot * rows + begin[q] + j * 16, 16), 16)
+                total = total + dxr[there].astype(jnp.float32)
             dxb[here] = total.astype(jnp.bfloat16)
             return c
 
-        lax.fori_loop(0, rows // 16, some, 0)
+        lax.fori_loop(0, length[q] // 16, some, 0)
+
+    def hand(de):
+        return pltpu.make_async_remote_copy(
+            src_ref=dxb.at[pl.ds(pl.multiple_of(z * rows + de * cap, 16), cap)],
+            dst_ref=hrecv.at[pl.ds(pl.multiple_of(y * cap, 16), cap)],
+            send_sem=h_send.at[de], recv_sem=h_recv.at[y],
+            device_id=(p - 1, lax.rem(y + de, experts), z), device_id_type=MESH,
+        )
 
     for k in range(n):
-        @pl.when(z == k)
+        @pl.when((z == k) & (p > 0))
         def _():
             for b in finish_order(k, n):
-                side = 1 if b > k else 0
-                taken(b)
-                add(b, [b])
-                running(k, b, side).start()
+                for q in (0, 1):
+                    taken(b, q)
+                    add(b, [b], q)
+                    running(k, b, q, 1 if b > k else 0).start()
             slots = ([k] if k > 0 else []) + ([n] if k < n - 1 else [])
-            for slot in slots:
-                taken(slot)
-            add(k, slots)
-
-    def hand(e):
-        return pltpu.make_async_remote_copy(
-            src_ref=dxb.at[pl.ds(pl.multiple_of(z * rows + e * cap, 16), cap)],
-            dst_ref=hrecv.at[pl.ds(pl.multiple_of(y * cap, 16), cap)],
-            send_sem=h_send.at[e], recv_sem=h_recv.at[y],
-            device_id=(p - 1, e, z), device_id_type=MESH,
-        )
-
-    @pl.when(p > 0)
-    def _():
-        for e in range(experts):
-            hand(e).start()
+            for q in (0, 1):
+                for slot in slots:
+                    taken(slot, q)
+                add(k, slots, q)
+                for de in (range(1, experts) if q else (0,)):
+                    hand(de).start()
 
     for de, dz in others:
         tell(de, dz).wait_recv()
@@ -312,15 +327,20 @@
             for b in range(n):
                 for side in sides(k):
                     if b == k or (b < k and side) or (b > k and not side):
-                        for t in range(2):
-                            forward(b, t, side).wait_send()
+                        for t, q in both:
+                            forward(b, t, q, side).wait_send()
+
+        @pl.when((z == k) & (p > 0))
+        def _():
+            for b in range(n):
                 if b != k:
-                    running(k, b, 1 if b > k else 0).wait_send()
+                    for q in (0, 1):
+                        running(k, b, q, 1 if b > k else 0).wait_send()
 
     @pl.when(p > 0)
     def _():
-        for e in range(experts):
-            hand(e).wait_send()
+        for de in range(experts):
+            hand(de).wait_send()
 
 
 def tables(route_col, experts, capacity, padded):
@@ -372,8 +392,8 @@
             pltpu.VMEM((n * rows, 128), full),
             pltpu.VMEM((n, rows, 128), full),
             dma((2, experts)), dma((2, experts)),
-            dma((2, n, 2)), dma((2, n, 2)),
-            dma((n,)), dma((n + 1,)),
+            dma((2, n, 2, 2)), dma((2, n, 2, 2)),
+            dma((n, 2)), dma((n + 1, 2)),
             dma((experts, n)), dma((experts, n)),
             dma((experts,)), dma((experts,)),
         ],

time: 296 us -> 255 us (0.86)
  Pallas kernels: 275 us -> 236 us
    pallas_call x1, Pallas kernels: 275 us -> 236 us  [per_device(): pl.pallas_call(functools.partial(kernel, (pipes, experts, n, cap, depth))...]
where the time goes in v2:
time: 255 us; the launch traced here: 254 us
  Pallas kernels  236 us (93%)
  local copies, waits for them, and re-layouts  10.1 us (4%)
  other arithmetic  5.35 us (2%)
    pallas_call x1, Pallas kernels, per_device(): pl.pallas_call(functools.partial(kernel, (pipes, experts, n, cap, depth))...  236 us
    unnamed x12, local copies, waits for them, and re-layouts  8.83 us
  transfers between devices with their start and end apart: 1, of which 0 were waited for; matrix products, arithmetic and copies ran while one was open for 2% of the time, Pallas kernels for 0%

profile of v2, /device:TPU:1, one launch (start us, length us, event | category | flops | bytes accessed | tf_op | source)
XLA Modules:
  0.0 254.0 jit_solution(7952423773773499400)
XLA Ops:
  0.6 2.0 collective-permute-start
  2.6 0.7 fusion.3
  3.4 0.8 copy.15
  4.1 0.2 reduce_window_sum.17
  4.3 0.8 select_reduce_fusion.2
  5.1 0.7 multiply_add_fusion.1
  5.8 0.6 fusion.tab_ref
  6.4 0.1 exponential_bitcast_fusion
  6.6 0.1 fusion.4
  6.7 0.6 convert_element_type.27.gate_ref
  7.3 0.0 collective-permute-done
  7.3 0.1 fusion.2
  7.4 0.2 reduce_window_sum.18
  7.6 0.2 select_reduce_fusion.1
  7.8 0.6 fusion.1.nxt_ref
  8.4 235.9 %shard_map.110 = (bf16[128,4096]{1,0:T(8,128)(2,1)}, bf16[192,4096]{1,0:T(8,128)(2,1)}, bf16[192,4096]{1,0:T(8,128)(2,1)}, bf16[192,4096]{1,0:T(8,128)(2,1)}, f32[160,128]{1,0:T(8,128)}) custom-call(bf16[128,4096]{1,0:T(8,128)(2,1)} %bitcast.21, bf16[128,4096]{1,0:T(8,128)(2,1)} %bitcast.22, f32[128,1]{1,0:T(8,128)} %convert_element_type.27.gate_ref, ...), custom_call_target="tpu_custom_call" | custom-call | tf_op jit(solution)/shard_map/pallas_call | solution.py:374
  244.3 0.0 copy-start.2
  244.3 1.1 slice_reduce_fusion
  245.4 0.1 select_reduce_fusion
  245.5 0.1 copy.16
  245.7 0.2 multiply_reduce_fusion
  245.9 0.1 subtract_multiply_fusion
  246.0 0.7 copy.17
  246.6 2.3 copy.22
  248.9 0.0 copy-done.2
  248.9 0.0 copy-start.1
  248.9 1.1 copy.23
  250.1 0.8 copy-done.1
  250.9 0.0 copy-start
  250.9 1.1 copy.24
  252.0 0.8 copy-done
  252.9 1.1 copy.25
  (2 shorter events, 0.0 us)
Async XLA Ops:
  0.6 6.7 %collective-permute-start = (s32[128]{0:T(128)}, s32[128]{0:T(128)S(1)}, u32[]{:S(2)}, u32[]{:S(2)}) collective-permute-start(s32[128]{0:T(128)} %bitcast.23), channel_id=1, source_target_pairs={{8,0},{16,8},{24,16},{9,1},{17,9},{25,17},{10,2},{18,10},{26,18},{... | collective-permute-start | bytes 1544 | tf_op jit(solution)/shard_map/ppermute | solution.py:363
  244.3 4.6 %copy-start.2 = (bf16[192,4096]{1,0:T(8,128)(2,1)S(1)}, bf16[192,4096]{1,0:T(8,128)(2,1)}, u32[]{:S(2)}) copy-start(bf16[192,4096]{1,0:T(8,128)(2,1)} %get-tuple-element.12) | copy-start | bytes 4718596
  248.9 2.0 copy-start.1
  250.9 2.0 copy-start

commit v3 on v2

--- a/solution.py
+++ b/solution.py
@@ -36,8 +36,8 @@
 def kernel(
     dims, x_ref, up_ref, gate_ref, tab_ref, nxt_ref, wg_ref, wu_ref, wd_ref,
     out_ref, gg_ref, gu_ref, gd_ref, s_ref,
-    stage, xb, yb, dxb, dxr, hrecv, act, pg, pu, sbuf, srecv,
-    ey_send, ey_recv, f_send, f_recv, r_send, r_recv, s_send, s_recv, h_send, h_recv,
+    xd, yd, tabs, stage, xb, yb, dxb, dxr, hrecv, act, pg, pu, sbuf, srecv,
+    t_send, t_recv, e_send, e_recv, f_send, f_recv, r_send, r_recv, s_send, s_recv, h_send, h_recv,
 ):
     pipes, experts, n, cap, depth = dims
     rows = experts * cap
@@ -69,39 +69,65 @@
     def piece(ref, b, q):
         return ref.at[pl.ds(pl.multiple_of(b * rows + begin[q], 16), length[q])]
 
-    tab = tab_ref[...]
     step = min(512, width)
-
-    def pack(t, buffer):
+    slots = stage.shape[0] // length[1]
+
+    def dense(ref, b):
+        return ref.at[pl.ds(pl.multiple_of(b * tokens, 16), tokens)]
+
+    def held(t, b, i):
+        return (dxb, b * rows + cap) if t == 0 else (stage, i % slots * length[1])
+
+    def exchange(t, b, i, de):
+        ref, off = held(t, b, i)
+        return pltpu.make_async_remote_copy(
+            src_ref=ref.at[pl.ds(pl.multiple_of(off + (de - 1) * cap, 16), cap)],
+            dst_ref=(xb, yb)[t].at[pl.ds(pl.multiple_of(b * rows + (experts - de) * cap, 16), cap)],
+            send_sem=e_send.at[t, i, de], recv_sem=e_recv.at[t, i, de],
+            device_id=(p, lax.rem(y + de, experts), z), device_id_type=MESH,
+        )
+
+    def pack(t, b, i):
+        if t and i >= slots:
+            for de in range(1, experts):
+                exchange(t, b, i - slots, de).wait_send()
+        source = dense((xd, yd)[t], b) if i or t else x_ref
+        ref, off = held(t, b, i)
+        tab = tabs[b]
+
         def tile(j, c):
             cols = pl.ds(pl.multiple_of(j * step, step), step)
-            if t == 0:
-                vals = x_ref[:, cols]
-            else:
-                vals = (gate_ref[...] * up_ref[:, cols].astype(jnp.float32)).astype(jnp.bfloat16)
-            stage[t, :, cols] = jnp.dot(tab, vals, preferred_element_type=jnp.float32).astype(jnp.bfloat16)
+            vals = jnp.dot(tab, source[:, cols], preferred_element_type=jnp.float32).astype(jnp.bfloat16)
+            (xb, yb)[t][pl.ds(pl.multiple_of(b * rows, 16), cap), cols] = vals[:cap]
+            ref[pl.ds(pl.multiple_of(off, 16), length[1]), cols] = vals[cap:]
             return c
 
         lax.fori_loop(0, width // step, tile, 0)
-
-    def exchange(t, buffer, de):
-        e = lax.rem(y + de, experts)
+        for de in range(1, experts):
+            exchange(t, b, i, de).start()
+
+    def scale(j, c):
+        cols = pl.ds(pl.multiple_of(j * step, step), step)
+        vals = (gate_ref[...] * up_ref[:, cols].astype(jnp.float32)).astype(jnp.bfloat16)
+        yd[pl.ds(pl.multiple_of(z * tokens, 16), tokens), cols] = vals
+        return c
+
+    def table_copy(dz):
         return pltpu.make_async_remote_copy(
-            src_ref=stage.at[t, pl.ds(pl.multiple_of(e * cap, 16), cap)],
-            dst_ref=buffer.at[pl.ds(pl.multiple_of(z * rows + (experts - de) * cap, 16), cap)],
-            send_sem=ey_send.at[t, de], recv_sem=ey_recv.at[t, de],
-            device_id=(p, e, z), device_id_type=MESH,
+            src_ref=tab_ref, dst_ref=tabs.at[z], send_sem=t_send.at[dz], recv_sem=t_recv.at[dz],
+            device_id=(p, y, lax.rem(z + dz, n)), device_id_type=MESH,
         )
 
-    pack(0, xb)
+    tabs[z] = tab_ref[...]
+    lax.fori_loop(0, width // step, scale, 0)
     around = (p > 0).astype(jnp.int32) + (p < pipes - 1).astype(jnp.int32)
     pl.semaphore_wait(barrier, len(others) + experts * around)
 
-    def forward(b, t, q, side):
-        buffer = (xb, yb)[t]
+    def forward(b, t, side, own=False):
+        there = dense((xd, yd)[t], b)
         return pltpu.make_async_remote_copy(
-            src_ref=piece(buffer, b, q), dst_ref=piece(buffer, b, q),
-            send_sem=f_send.at[side, b, t, q], recv_sem=f_recv.at[side, b, t, q],
+            src_ref=x_ref if own and t == 0 else there, dst_ref=there,
+            send_sem=f_send.at[side, b, t], recv_sem=f_recv.at[side, b, t],
             device_id=(p, y, z + (1 if side else -1)), device_id_type=MESH,
         )
 
@@ -117,11 +143,11 @@
         whole = piece(dxr, slot, q)
         pltpu.make_async_copy(whole, whole, r_recv.at[slot, q]).wait()
 
-    def arrive(k, b, t, q):
+    def arrive(k, b, t):
         side = 1 if b < k else 0
-        forward(b, t, q, side).wait_recv()
+        forward(b, t, side).wait_recv()
         if side and k < n - 1 or not side and k > 0:
-            forward(b, t, q, side).start()
+            forward(b, t, side).start()
 
     def near_end(k, side):
         return n > 2 and (side and k == n - 2 or not side and k == 1)
@@ -129,25 +155,15 @@
     def sides(k):
         return ([1] if k < n - 1 else []) + ([0] if k > 0 else [])
 
-    def depart(t, q):
+    for t in range(2):
         for k in range(n):
             @pl.when(z == k)
             def _():
                 for side in sides(k):
                     if t == 0 or not near_end(k, side):
-                        forward(k, t, q, side).start()
-
-    for t, buffer in ((0, xb), (1, yb)):
-        if t:
-            pack(1, yb)
-        for de in range(1, experts):
-            exchange(t, buffer, de).start()
-        buffer[pl.ds(pl.multiple_of(z * rows, 16), cap)] = stage[t, pl.ds(pl.multiple_of(y * cap, 16), cap)]
-        depart(t, 0)
-    for t, buffer in ((0, xb), (1, yb)):
-        for de in range(1, experts):
-            exchange(t, buffer, de).wait_recv()
-        depart(t, 1)
+                        forward(k, t, side, True).start()
+    for dz in range(1, n):
+        table_copy(dz).start()
 
     def work(b, start, size):
         off = pl.multiple_of(b * rows + start, 16)
@@ -186,62 +202,123 @@
         lax.fori_loop(0, width // step, back, 0)
 
     orders = [compute_order(k, n) for k in range(n)]
-    both = ((0, 0), (1, 0), (0, 1), (1, 1))
-    for i in range(n):
+    def place(ks, i):
         b = 0
-        for k in range(n):
+        for k in ks:
             b = b + (z == k).astype(jnp.int32) * orders[k][i]
-        last = n > 1 and i == n - 1
-        for part in ((0, 1) if last else (None,)):
-            items = [item for item in both if part is None or item[1] == part]
-            for k in range(n) if i else ():
-                @pl.when(z == k)
-                def _():
-                    c = orders[k][i]
-                    if k in (0, n - 1):
-                        for t, q in items:
-                            arrive(k, c, t, q)
-                    else:
-                        d = abs(c - k)
-                        pair = [e for e in (k - d, k + d) if 0 <= e < n]
-                        if last and len(pair) == 1 or not last and all(orders[k].index(e) >= i for e in pair):
-                            for t, q in items:
-                                for e in pair:
-                                    arrive(k, e, t, q)
-                        if last and part == 1:
-                            for side in sides(k):
-                                if near_end(k, side):
-                                    forward(k, 1, 0, side).start()
-            if part is None:
-                work(b, 0, rows)
-            else:
-                work(b, begin[part], length[part])
-            if last and part == 1:
-                for k in range(n):
-                    for side in sides(k):
-                        if near_end(k, side):
-                            @pl.when(z == k)
-                            def _():
-                                forward(k, 1, 1, side).start()
-            if i:
-                for k in (0, n - 1):
+        return b
+
+    def come(ks, t, indices):
+        for k in ks:
+            @pl.when(z == k)
+            def _():
+                for i in indices:
+                    arrive(k, orders[k][i], t)
+
+    def join(b, i):
+        for de in range(1, experts):
+            exchange(0, b, i, de).wait_send()
+            for t in range(2):
+                exchange(t, b, i, de).wait_recv()
+
+    def part(ks, i, q):
+        b = place(ks, i)
+        if q:
+            join(b, i)
+        work(b, begin[q], length[q])
+        if i:
+            for k in ks:
+                if k in (0, n - 1):
                     @pl.when((z == k) & (p > 0))
                     def _():
-                        for q in (0, 1) if part is None else (part,):
-                            running(k, orders[k][i], q, 0 if k else 1).start()
+                        running(k, orders[k][i], q, 0 if k else 1).start()
+
+    def whole(ks, i):
+        b = place(ks, i)
+        join(b, i)
+        work(b, 0, rows)
+
+    def tables_here():
+        for dz in range(1, n):
+            table_copy(dz).wait_recv()
+
+    ends, middle = sorted({0, n - 1}), list(range(1, n - 1))
+
+    @pl.when((z == 0) | (z == n - 1))
+    def _():
+        for t in range(2):
+            pack(t, place(ends, 0), 0)
+        tables_here()
+        if n > 2:
+            come(ends, 0, [n - 1])
+            pack(0, place(ends, n - 1), n - 1)
+        for i in range(1, n - 1):
+            for t in range(2):
+                come(ends, t, [i])
+                pack(t, place(ends, i), i)
+            if i == 1:
+                whole(ends, 0)
+            part(ends, i, 0)
+            part(ends, i, 1)
+        for t in range(2) if n == 2 else (1,):
+            come(ends, t, [n - 1])
+            pack(t, place(ends, n - 1), n - 1)
+        if n == 2:
+            whole(ends, 0)
+        part(ends, n - 1, 0)
+        part(ends, n - 1, 1)
+
+    if middle:
+        @pl.when((z > 0) & (z < n - 1))
+        def _():
+            def release():
+                for k in middle:
+                    @pl.when(z == k)
+                    def _():
+                        for side in sides(k):
+                            if near_end(k, side):
+                                forward(k, 1, side, True).start()
+
+            for t in range(2):
+                pack(t, place(middle, 0), 0)
+            tables_here()
+            for t in range(2):
+                come(middle, t, [1, 2])
+                for i in (1, 2):
+                    pack(t, place(middle, i), i)
+            if n == 3:
+                release()
+            whole(middle, 0)
+            due = [1, 2]
+            for i in range(3, n):
+                come(middle, 0, [i])
+                pack(0, place(middle, i), i)
+                for c in due:
+                    whole(middle, c)
+                come(middle, 1, [i])
+                if i == n - 1:
+                    release()
+                pack(1, place(middle, i), i)
+                due = [i]
+            for c in due:
+                if c == n - 1:
+                    part(middle, c, 0)
+                    part(middle, c, 1)
+                else:
+                    whole(middle, c)
 
     def tell(de, dz):
         ey, ez = peer(de, dz)
         return pltpu.make_async_remote_copy(
             src_ref=sbuf.at[pl.ds(pl.multiple_of(ez * rows + de * cap, 16), cap)],
-            dst_ref=srecv.at[z, pl.ds(pl.multiple_of(y * cap, 16), cap)],
+            dst_ref=srecv.at[z, pl.ds((experts - de) % experts * cap, cap)],
             send_sem=s_send.at[de, dz], recv_sem=s_recv.at[de, dz],
             device_id=(p, ey, ez), device_id_type=MESH,
         )
 
     for de, dz in others:
         tell(de, dz).start()
-    srecv[z, pl.ds(pl.multiple_of(y * cap, 16), cap)] = sbuf[
+    srecv[z, :cap] = sbuf[
         pl.ds(pl.multiple_of(z * rows, 16), cap)
     ]
 
@@ -270,8 +347,8 @@
     def hand(de):
         return pltpu.make_async_remote_copy(
             src_ref=dxb.at[pl.ds(pl.multiple_of(z * rows + de * cap, 16), cap)],
-            dst_ref=hrecv.at[pl.ds(pl.multiple_of(y * cap, 16), cap)],
-            send_sem=h_send.at[de], recv_sem=h_recv.at[y],
+            dst_ref=hrecv.at[pl.ds((experts - de) % experts * cap, cap)],
+            send_sem=h_send.at[de], recv_sem=h_recv.at[de],
             device_id=(p - 1, lax.rem(y + de, experts), z), device_id_type=MESH,
         )
 
@@ -283,11 +360,11 @@
                     taken(b, q)
                     add(b, [b], q)
                     running(k, b, q, 1 if b > k else 0).start()
-            slots = ([k] if k > 0 else []) + ([n] if k < n - 1 else [])
+            ends_in = ([k] if k > 0 else []) + ([n] if k < n - 1 else [])
             for q in (0, 1):
-                for slot in slots:
+                for slot in ends_in:
                     taken(slot, q)
-                add(k, slots, q)
+                add(k, ends_in, q)
                 for de in (range(1, experts) if q else (0,)):
                     hand(de).start()
 
@@ -301,7 +378,7 @@
     @pl.when(p < pipes - 1)
     def _():
         for e in range(experts):
-            pltpu.make_async_copy(hrecv.at[pl.ds(e * cap, cap)], hrecv.at[pl.ds(e * cap, cap)], h_recv.at[e]).wait()
+            hand(e).wait_recv()
 
         def tile(j, c):
             cols = pl.ds(pl.multiple_of(j * step, step), step)
@@ -316,9 +393,11 @@
     def _():
         out_ref[...] = jnp.zeros_like(out_ref)
 
-    for t, buffer in ((0, xb), (1, yb)):
+    for i in range(max(0, n - slots), n):
         for de in range(1, experts):
-            exchange(t, buffer, de).wait_send()
+            exchange(1, 0, i, de).wait_send()
+    for dz in range(1, n):
+        table_copy(dz).wait_send()
     for de, dz in others:
         tell(de, dz).wait_send()
     for k in range(n):
@@ -327,8 +406,8 @@
             for b in range(n):
                 for side in sides(k):
                     if b == k or (b < k and side) or (b > k and not side):
-                        for t, q in both:
-                            forward(b, t, q, side).wait_send()
+                        for t in range(2):
+                            forward(b, t, side, b == k).wait_send()
 
         @pl.when((z == k) & (p > 0))
         def _():
@@ -343,12 +422,12 @@
             hand(de).wait_send()
 
 
-def tables(route_col, experts, capacity, padded):
+def tables(route_col, experts, padded):
     expert_ids = jnp.arange(experts, dtype=jnp.int32)
     onehot = (route_col[:, None] == expert_ids).astype(jnp.int32)
     earlier = jnp.cumsum(onehot, axis=0) - onehot
     slot = jnp.sum(onehot * earlier, axis=1)
-    position = route_col * padded + slot
+    position = (route_col - lax.axis_index("expert") + experts) % experts * padded + slot
     return (jnp.arange(experts * padded, dtype=jnp.int32)[:, None] == position[None, :])
 
 
@@ -361,8 +440,8 @@
     rows = experts * cap
     route_col = routes[0, :, 0]
     behind = lax.ppermute(route_col, "pipe", [(i + 1, i) for i in range(pipes - 1)])
-    table = tables(route_col, experts, capacity, cap)
-    following = tables(behind, experts, capacity, cap).astype(jnp.bfloat16)
+    table = tables(route_col, experts, cap)
+    following = tables(behind, experts, cap).astype(jnp.bfloat16)
     raised = jnp.exp(router_scores[0])
     weights = raised / jnp.sum(raised, axis=1, keepdims=True)
     gate = lax.optimization_barrier(weights[:, 0:1].astype(jnp.bfloat16)).astype(jnp.float32)
@@ -380,7 +459,10 @@
         in_specs=[vmem] * 8,
         out_specs=(vmem,) * 5,
         scratch_shapes=[
-            pltpu.VMEM((2, rows, width), half),
+            pltpu.VMEM((n * tokens, width), half),
+            pltpu.VMEM((n * tokens, width), half),
+            pltpu.VMEM((n, rows, tokens), half),
+            pltpu.VMEM((min(n, max(1, 320 // (rows - cap))) * (rows - cap), width), half),
             pltpu.VMEM((n * rows, width), half),
             pltpu.VMEM((n * rows, width), half),
             pltpu.VMEM((n * rows, width), half),
@@ -391,14 +473,15 @@
             pltpu.VMEM((n * rows, depth), half),
             pltpu.VMEM((n * rows, 128), full),
             pltpu.VMEM((n, rows, 128), full),
-            dma((2, experts)), dma((2, experts)),
-            dma((2, n, 2, 2)), dma((2, n, 2, 2)),
+            dma((n,)), dma((n,)),
+            dma((2, n, experts)), dma((2, n, experts)),
+            dma((2, n, 2)), dma((2, n, 2)),
             dma((n, 2)), dma((n + 1, 2)),
             dma((experts, n)), dma((experts, n)),
             dma((experts,)), dma((experts,)),
         ],
         compiler_params=pltpu.CompilerParams(
-            collective_id=0, has_side_effects=True, vmem_limit_bytes=62 * 1024 * 1024
+            collective_id=0, has_side_effects=True, vmem_limit_bytes=63 * 1024 * 1024
         ),
     )(
         inputs[0], cotangent[0], gate, table.astype(half), following,

time: 255 us -> 261 us (1.024)
  Pallas kernels: 236 us -> 243 us
    pallas_call x1, Pallas kernels: 236 us -> 243 us  [per_device(): pl.pallas_call(functools.partial(kernel, (pipes, experts, n, cap, depth))...]
where the time goes in v3:
time: 261 us
  Pallas kernels  243 us (93%)
  local copies, waits for them, and re-layouts  10.1 us (4%)
  other arithmetic  5.38 us (2%)
    pallas_call x1, Pallas kernels, per_device(): pl.pallas_call(functools.partial(kernel, (pipes, experts, n, cap, depth))...  243 us
    unnamed x12, local copies, waits for them, and re-layouts  8.83 us
  transfers between devices with their start and end apart: 1, of which 0 were waited for; matrix products, arithmetic and copies ran while one was open for 2% of the time, Pallas kernels for 0%

profile of v3, /device:TPU:1, one launch (start us, length us, event | category | flops | bytes accessed | tf_op | source)
XLA Modules:
  0.0 260.9 jit_solution(14225474885396046516)
XLA Ops:
  0.6 2.0 collective-permute-start
  2.6 0.7 fusion.3
  3.4 0.8 copy.15
  4.1 0.2 reduce_window_sum.17
  4.3 0.8 select_reduce_fusion.2
  5.2 0.7 fusion.6
  5.8 0.6 fusion.tab_ref
  6.5 0.1 exponential_bitcast_fusion
  6.6 0.1 fusion.4
  6.7 0.6 convert_element_type.27.gate_ref
  7.3 0.0 collective-permute-done
  7.3 0.1 fusion.2
  7.4 0.2 reduce_window_sum.18
  7.6 0.2 select_reduce_fusion.1
  7.8 0.6 fusion.1.nxt_ref
  8.4 242.8 %shard_map.110 = (bf16[128,4096]{1,0:T(8,128)(2,1)}, bf16[192,4096]{1,0:T(8,128)(2,1)}, bf16[192,4096]{1,0:T(8,128)(2,1)}, bf16[192,4096]{1,0:T(8,128)(2,1)}, f32[160,128]{1,0:T(8,128)}) custom-call(bf16[128,4096]{1,0:T(8,128)(2,1)} %bitcast.21, bf16[128,4096]{1,0:T(8,128)(2,1)} %bitcast.22, f32[128,1]{1,0:T(8,128)} %convert_element_type.27.gate_ref, ...), custom_call_target="tpu_custom_call" | custom-call | tf_op jit(solution)/shard_map/pallas_call | solution.py:453
  251.2 0.0 copy-start.2
  251.2 1.1 slice_reduce_fusion
  252.4 0.1 select_reduce_fusion
  252.5 0.1 copy.16
  252.6 0.2 multiply_reduce_fusion
  252.8 0.1 subtract_multiply_fusion
  252.9 0.7 copy.17
  253.5 2.3 copy.22
  255.8 0.0 copy-done.2
  255.8 0.0 copy-start.1
  255.8 1.1 copy.23
  257.0 0.8 copy-done.1
  257.8 0.0 copy-start
  257.8 1.1 copy.24
  259.0 0.8 copy-done
  259.8 1.1 copy.25
  (2 shorter events, 0.0 us)
Async XLA Ops:
  0.6 6.7 %collective-permute-start = (s32[128]{0:T(128)}, s32[128]{0:T(128)S(1)}, u32[]{:S(2)}, u32[]{:S(2)}) collective-permute-start(s32[128]{0:T(128)} %bitcast.23), channel_id=1, source_target_pairs={{8,0},{16,8},{24,16},{9,1},{17,9},{25,17},{10,2},{18,10},{26,18},{... | collective-permute-start | bytes 1544 | tf_op jit(solution)/shard_map/ppermute | solution.py:442
  251.2 4.6 %copy-start.2 = (bf16[192,4096]{1,0:T(8,128)(2,1)S(1)}, bf16[192,4096]{1,0:T(8,128)(2,1)}, u32[]{:S(2)}) copy-start(bf16[192,4096]{1,0:T(8,128)(2,1)} %get-tuple-element.12) | copy-start | bytes 4718596
  255.8 2.0 copy-start.1
  257.8 2.0 copy-start

commit v4 on v2

--- a/solution.py
+++ b/solution.py
@@ -34,9 +34,9 @@
 
 
 def kernel(
-    dims, x_ref, up_ref, gate_ref, tab_ref, nxt_ref, wg_ref, wu_ref, wd_ref,
-    out_ref, gg_ref, gu_ref, gd_ref, s_ref,
-    stage, xb, yb, dxb, dxr, hrecv, act, pg, pu, sbuf, srecv,
+    dims, x_ref, up_ref, gate_ref, tab_ref, wg_ref, wu_ref, wd_ref,
+    hrecv, gg_ref, gu_ref, gd_ref, s_ref,
+    stage, xb, yb, dxb, dxr, act, pg, pu, turned, sbuf, srecv,
     ey_send, ey_recv, f_send, f_recv, r_send, r_recv, s_send, s_recv, h_send, h_recv,
 ):
     pipes, experts, n, cap, depth = dims
@@ -192,20 +192,25 @@
         for k in range(n):
             b = b + (z == k).astype(jnp.int32) * orders[k][i]
         last = n > 1 and i == n - 1
-        for part in ((0, 1) if last else (None,)):
+        for part in ((0, 1) if i else (None,)):
             items = [item for item in both if part is None or item[1] == part]
-            for k in range(n) if i else ():
+            for k in range(n):
                 @pl.when(z == k)
                 def _():
                     c = orders[k][i]
-                    if k in (0, n - 1):
+                    if i == 0:
+                        if 0 < k < n - 1:
+                            for t in range(2):
+                                for e in (k - 1, k + 1):
+                                    arrive(k, e, t, 0)
+                    elif k in (0, n - 1):
                         for t, q in items:
                             arrive(k, c, t, q)
                     else:
                         d = abs(c - k)
                         pair = [e for e in (k - d, k + d) if 0 <= e < n]
                         if last and len(pair) == 1 or not last and all(orders[k].index(e) >= i for e in pair):
-                            for t, q in items:
+                            for t, q in items if i > 1 or part else ():
                                 for e in pair:
                                     arrive(k, e, t, q)
                         if last and part == 1:
@@ -245,12 +250,15 @@
         pl.ds(pl.multiple_of(z * rows, 16), cap)
     ]
 
+    for m, ref in enumerate((act, pg, pu)):
+        turned[m] = ref[...].T
+
     def weights(j, c):
         cols = pl.ds(pl.multiple_of(j * step, step), step)
         yt, xt = yb[:, cols], xb[:, cols]
-        gd_ref[:, cols] = lax.dot_general(act[...], yt, TN, preferred_element_type=jnp.float32).astype(jnp.bfloat16)
-        gg_ref[:, cols] = lax.dot_general(pg[...], xt, TN, preferred_element_type=jnp.float32).astype(jnp.bfloat16)
-        gu_ref[:, cols] = lax.dot_general(pu[...], xt, TN, preferred_element_type=jnp.float32).astype(jnp.bfloat16)
+        gd_ref[:, cols] = jnp.dot(turned[0], yt, preferred_element_type=jnp.float32).astype(jnp.bfloat16)
+        gg_ref[:, cols] = jnp.dot(turned[1], xt, preferred_element_type=jnp.float32).astype(jnp.bfloat16)
+        gu_ref[:, cols] = jnp.dot(turned[2], xt, preferred_element_type=jnp.float32).astype(jnp.bfloat16)
         return c
 
     lax.fori_loop(0, width // step, weights, 0)
@@ -303,18 +311,9 @@
         for e in range(experts):
             pltpu.make_async_copy(hrecv.at[pl.ds(e * cap, cap)], hrecv.at[pl.ds(e * cap, cap)], h_recv.at[e]).wait()
 
-        def tile(j, c):
-            cols = pl.ds(pl.multiple_of(j * step, step), step)
-            out_ref[:, cols] = lax.dot_general(
-                nxt_ref[...], hrecv[:, cols], TN, preferred_element_type=jnp.float32
-            ).astype(jnp.bfloat16)
-            return c
-
-        lax.fori_loop(0, width // step, tile, 0)
-
     @pl.when(p == pipes - 1)
     def _():
-        out_ref[...] = jnp.zeros_like(out_ref)
+        hrecv[...] = jnp.zeros_like(hrecv)
 
     for t, buffer in ((0, xb), (1, yb)):
         for de in range(1, experts):
@@ -371,13 +370,13 @@
     half, full = jnp.bfloat16, jnp.float32
     dma = pltpu.SemaphoreType.DMA
     grad = jax.ShapeDtypeStruct((depth, width), half)
-    handed, grad_gate, grad_up, grad_down, sums = pl.pallas_call(
+    returned, grad_gate, grad_up, grad_down, sums = pl.pallas_call(
         functools.partial(kernel, (pipes, experts, n, cap, depth)),
         out_shape=(
-            jax.ShapeDtypeStruct((tokens, width), half), grad, grad, grad,
+            jax.ShapeDtypeStruct((rows, width), half), grad, grad, grad,
             jax.ShapeDtypeStruct((rows, 128), full),
         ),
-        in_specs=[vmem] * 8,
+        in_specs=[vmem] * 7,
         out_specs=(vmem,) * 5,
         scratch_shapes=[
             pltpu.VMEM((2, rows, width), half),
@@ -385,10 +384,10 @@
             pltpu.VMEM((n * rows, width), half),
             pltpu.VMEM((n * rows, width), half),
             pltpu.VMEM(((n + 1) * rows, width), half),
-            pltpu.VMEM((rows, width), half),
             pltpu.VMEM((n * rows, depth), half),
             pltpu.VMEM((n * rows, depth), half),
             pltpu.VMEM((n * rows, depth), half),
+            pltpu.VMEM((3, depth, n * rows), half),
             pltpu.VMEM((n * rows, 128), full),
             pltpu.VMEM((n, rows, 128), full),
             dma((2, experts)), dma((2, experts)),
@@ -401,9 +400,10 @@
             collective_id=0, has_side_effects=True, vmem_limit_bytes=62 * 1024 * 1024
         ),
     )(
-        inputs[0], cotangent[0], gate, table.astype(half), following,
+        inputs[0], cotangent[0], gate, table.astype(half),
         w_gate[0, 0], w_up[0, 0], w_down[0, 0],
     )
+    handed = lax.dot_general(following, returned, TN, preferred_element_type=full).astype(half)
     gate_grad = jnp.sum(jnp.where(table, sums[:, 0:1], 0.0), axis=0)[:, None] / gate
     is_first = (jnp.arange(router_scores.shape[2]) == 0).astype(full)
     score_grad = gate_grad * weights[:, 0:1] * (is_first - weights)

time: 255 us -> 246 us (0.965)
  Pallas kernels: 236 us -> 228 us
  matrix products: 0 us -> 2.78 us
    pallas_call x1, Pallas kernels: 236 us -> 228 us  [per_device(): pl.pallas_call(functools.partial(kernel, (pipes, experts, n, cap, depth))...]
    dot_general x0 -> x1, matrix products: none -> 2.78 us  [per_device(): lax.dot_general(following, returned, TN, preferred_element_type=full)]
    unnamed x12 -> x11, local copies, waits for them, and re-layouts: 8.83 us -> 6.55 us
  transfers between devices with their start and end apart: 1 -> 1, of which waited for: 0 -> 0; matrix products, arithmetic and copies ran while one was open for 2% -> 3% of each run, Pallas kernels for 0% -> 93%
where the time goes in v4:
time: 246 us
  Pallas kernels  228 us (93%)
  local copies, waits for them, and re-layouts  7.77 us (3%)
  other arithmetic  4.72 us (2%)
  matrix products  2.78 us (1%)
    pallas_call x1, Pallas kernels, per_device(): pl.pallas_call(functools.partial(kernel, (pipes, experts, n, cap, depth))...  228 us
    unnamed x11, local copies, waits for them, and re-layouts  6.55 us
  transfers between devices with their start and end apart: 1, of which 0 were waited for; matrix products, arithmetic and copies ran while one was open for 3% of the time, Pallas kernels for 93%

profile of v4, /device:TPU:1, one launch (start us, length us, event | category | flops | bytes accessed | tf_op | source)
XLA Modules:
  0.0 245.7 jit_solution(10852531042300353234)
XLA Ops:
  0.6 2.0 collective-permute-start
  2.6 0.7 fusion.3
  3.4 0.8 copy.15
  4.2 0.2 reduce_window_sum.17
  4.3 0.8 select_reduce_fusion.2
  5.2 0.7 multiply_add_fusion.1
  5.8 0.6 fusion.1.tab_ref
  6.5 0.1 exponential_bitcast_fusion
  6.6 0.1 fusion.5
  6.7 0.6 convert_element_type.28.gate_ref
  7.3 227.7 %shard_map.110 = (bf16[160,4096]{1,0:T(8,128)(2,1)}, bf16[192,4096]{1,0:T(8,128)(2,1)}, bf16[192,4096]{1,0:T(8,128)(2,1)}, bf16[192,4096]{1,0:T(8,128)(2,1)}, f32[160,128]{1,0:T(8,128)}) custom-call(bf16[128,4096]{1,0:T(8,128)(2,1)} %bitcast.22, bf16[128,4096]{1,0:T(8,128)(2,1)} %bitcast.23, f32[128,1]{1,0:T(8,128)} %convert_element_type.28.gate_ref, ...), custom_call_target="tpu_custom_call" | custom-call | tf_op jit(solution)/shard_map/pallas_call | solution.py:373
  235.1 0.0 copy-start.2
  235.1 1.1 slice_reduce_fusion
  236.2 0.1 select_reduce_fusion
  236.3 0.1 copy.16
  236.4 0.2 multiply_reduce_fusion
  236.6 0.1 subtract_multiply_fusion
  236.7 0.7 copy.17
  237.4 0.0 collective-permute-done
  237.4 0.1 fusion.2
  237.5 0.2 reduce_window_sum.18
  237.6 0.2 select_reduce_fusion.1
  237.8 2.8 %fusion = bf16[1,128,4096]{2,1,0:T(8,128)(2,1)} fusion(bf16[160,4096]{1,0:T(8,128)(2,1)} %get-tuple-element.11, s32[128]{0:T(128)S(1)} %multiply_add_fusion), kind=kOutput, calls=%fused_computation.1 | convolution fusion | flops 168316928 | bytes 2359808 | tf_op jit(solution)/shard_map/dot_general | solution.py:406
  240.6 0.0 copy-done.2
  240.6 0.0 copy-start.1
  240.6 1.1 copy.21
  241.8 0.8 copy-done.1
  242.6 0.0 copy-start
  242.6 1.1 copy.22
  243.7 0.8 copy-done
  244.6 1.1 copy.23
  (2 shorter events, 0.0 us)
Async XLA Ops:
  0.6 236.8 %collective-permute-start = (s32[128]{0:T(128)}, s32[128]{0:T(128)S(1)}, u32[]{:S(2)}, u32[]{:S(2)}) collective-permute-start(s32[128]{0:T(128)} %bitcast.24), channel_id=1, source_target_pairs={{8,0},{16,8},{24,16},{9,1},{17,9},{25,17},{10,2},{18,10},{26,18},{... | collective-permute-start | bytes 1544 | tf_op jit(solution)/shard_map/ppermute | solution.py:362
  235.1 5.6 %copy-start.2 = (bf16[192,4096]{1,0:T(8,128)(2,1)S(1)}, bf16[192,4096]{1,0:T(8,128)(2,1)}, u32[]{:S(2)}) copy-start(bf16[192,4096]{1,0:T(8,128)(2,1)} %get-tuple-element.12) | copy-start | bytes 4718596
  240.6 2.0 copy-start.1
  242.6 2.0 copy-start

commit v5 on v4

--- a/solution.py
+++ b/solution.py
@@ -34,8 +34,9 @@
 
 
 def kernel(
-    dims, x_ref, up_ref, gate_ref, tab_ref, wg_ref, wu_ref, wd_ref,
-    hrecv, gg_ref, gu_ref, gd_ref, s_ref,
+    dims, x_ref, up_ref, gate_ref, tab_ref, wg_hbm, wu_hbm, wd_hbm,
+    hrecv, gg_hbm, gu_hbm, gd_hbm, s_ref,
+    wg_ref, wu_ref, wd_ref, gg_ref, gu_ref, gd_ref, w_sem, g_sem,
     stage, xb, yb, dxb, dxr, act, pg, pu, turned, sbuf, srecv,
     ey_send, ey_recv, f_send, f_recv, r_send, r_recv, s_send, s_recv, h_send, h_recv,
 ):
@@ -49,6 +50,16 @@
 
     others = [(de, dz) for de in range(experts) for dz in range(n) if (de, dz) != (0, 0)]
 
+    reads = [
+        pltpu.make_async_copy(src, dst, w_sem.at[m])
+        for m, (src, dst) in enumerate(((wg_hbm, wg_ref), (wu_hbm, wu_ref), (wd_hbm, wd_ref)))
+    ]
+    writes = [
+        pltpu.make_async_copy(src, dst, g_sem.at[m])
+        for m, (src, dst) in enumerate(((gg_ref, gg_hbm), (gu_ref, gu_hbm), (gd_ref, gd_hbm)))
+    ]
+    for copy in reads:
+        copy.start()
     barrier = pltpu.get_barrier_semaphore()
     for de, dz in others:
         ey, ez = peer(de, dz)
@@ -186,6 +197,8 @@
         lax.fori_loop(0, width // step, back, 0)
 
     orders = [compute_order(k, n) for k in range(n)]
+    for copy in reads:
+        copy.wait()
     both = ((0, 0), (1, 0), (0, 1), (1, 1))
     for i in range(n):
         b = 0
@@ -262,6 +275,8 @@
         return c
 
     lax.fori_loop(0, width // step, weights, 0)
+    for copy in writes:
+        copy.start()
 
     def add(b, slots, q):
         def some(j, c):
@@ -315,6 +330,8 @@
     def _():
         hrecv[...] = jnp.zeros_like(hrecv)
 
+    for copy in writes:
+        copy.wait()
     for t, buffer in ((0, xb), (1, yb)):
         for de in range(1, experts):
             exchange(t, buffer, de).wait_send()
@@ -366,7 +383,7 @@
     weights = raised / jnp.sum(raised, axis=1, keepdims=True)
     gate = lax.optimization_barrier(weights[:, 0:1].astype(jnp.bfloat16)).astype(jnp.float32)
 
-    vmem = pl.BlockSpec(memory_space=pltpu.VMEM)
+    vmem, hbm = pl.BlockSpec(memory_space=pltpu.VMEM), pl.BlockSpec(memory_space=pl.ANY)
     half, full = jnp.bfloat16, jnp.float32
     dma = pltpu.SemaphoreType.DMA
     grad = jax.ShapeDtypeStruct((depth, width), half)
@@ -376,9 +393,11 @@
             jax.ShapeDtypeStruct((rows, width), half), grad, grad, grad,
             jax.ShapeDtypeStruct((rows, 128), full),
         ),
-        in_specs=[vmem] * 7,
-        out_specs=(vmem,) * 5,
+        in_specs=[vmem] * 4 + [hbm] * 3,
+        out_specs=(vmem, hbm, hbm, hbm, vmem),
         scratch_shapes=[
+            *[pltpu.VMEM((depth, width), half)] * 6,
+            dma((3,)), dma((3,)),
             pltpu.VMEM((2, rows, width), half),
             pltpu.VMEM((n * rows, width), half),
             pltpu.VMEM((n * rows, width), half),

time: 246 us -> 243 us (0.988)
  Pallas kernels: 228 us -> 225 us
    pallas_call x1, Pallas kernels: 228 us -> 225 us  [per_device(): pl.pallas_call(functools.partial(kernel, (pipes, experts, n, cap, depth))...]
where the time goes in v5:
time: 243 us
  Pallas kernels  225 us (93%)
  local copies, waits for them, and re-layouts  7.77 us (3%)
  other arithmetic  4.72 us (2%)
  matrix products  2.78 us (1%)
    pallas_call x1, Pallas kernels, per_device(): pl.pallas_call(functools.partial(kernel, (pipes, experts, n, cap, depth))...  225 us
    unnamed x11, local copies, waits for them, and re-layouts  6.55 us
  transfers between devices with their start and end apart: 1, of which 0 were waited for; matrix products, arithmetic and copies ran while one was open for 3% of the time, Pallas kernels for 93%

profile of v5, /device:TPU:1, one launch (start us, length us, event | category | flops | bytes accessed | tf_op | source)
XLA Modules:
  0.0 242.8 jit_solution(280239519956882533)
XLA Ops:
  0.6 2.0 collective-permute-start
  2.6 0.7 fusion.3
  3.4 0.8 copy.15
  4.2 0.2 reduce_window_sum.17
  4.3 0.8 select_reduce_fusion.2
  5.2 0.7 multiply_add_fusion.1
  5.8 0.6 fusion.1.tab_ref
  6.5 0.1 exponential_bitcast_fusion
  6.6 0.1 fusion.5
  6.7 0.6 convert_element_type.28.gate_ref
  7.3 224.9 %shard_map.110 = (bf16[160,4096]{1,0:T(8,128)(2,1)}, bf16[192,4096]{1,0:T(8,128)(2,1)}, bf16[192,4096]{1,0:T(8,128)(2,1)}, bf16[192,4096]{1,0:T(8,128)(2,1)}, f32[160,128]{1,0:T(8,128)}) custom-call(bf16[128,4096]{1,0:T(8,128)(2,1)} %bitcast.22, bf16[128,4096]{1,0:T(8,128)(2,1)} %bitcast.23, f32[128,1]{1,0:T(8,128)} %convert_element_type.28.gate_ref, ...), custom_call_target="tpu_custom_call" | custom-call | tf_op jit(solution)/shard_map/pallas_call | solution.py:390
  232.2 0.0 copy-start.2
  232.2 1.1 slice_reduce_fusion
  233.3 0.1 select_reduce_fusion
  233.4 0.1 copy.16
  233.5 0.2 multiply_reduce_fusion
  233.7 0.1 subtract_multiply_fusion
  233.9 0.7 copy.17
  234.5 0.0 collective-permute-done
  234.5 0.1 fusion.2
  234.6 0.2 reduce_window_sum.18
  234.8 0.2 select_reduce_fusion.1
  235.0 2.8 %fusion = bf16[1,128,4096]{2,1,0:T(8,128)(2,1)} fusion(bf16[160,4096]{1,0:T(8,128)(2,1)} %get-tuple-element.11, s32[128]{0:T(128)S(1)} %multiply_add_fusion), kind=kOutput, calls=%fused_computation.1 | convolution fusion | flops 168316928 | bytes 2359808 | tf_op jit(solution)/shard_map/dot_general | solution.py:425
  237.7 0.0 copy-done.2
  237.7 0.0 copy-start.1
  237.8 1.1 copy.21
  238.9 0.8 copy-done.1
  239.7 0.0 copy-start
  239.7 1.1 copy.22
  240.9 0.8 copy-done
  241.7 1.1 copy.23
  (2 shorter events, 0.0 us)
Async XLA Ops:
  0.6 233.9 %collective-permute-start = (s32[128]{0:T(128)}, s32[128]{0:T(128)S(1)}, u32[]{:S(2)}, u32[]{:S(2)}) collective-permute-start(s32[128]{0:T(128)} %bitcast.24), channel_id=1, source_target_pairs={{8,0},{16,8},{24,16},{9,1},{17,9},{25,17},{10,2},{18,10},{26,18},{... | collective-permute-start | bytes 1544 | tf_op jit(solution)/shard_map/ppermute | solution.py:379
  232.2 5.6 %copy-start.2 = (bf16[192,4096]{1,0:T(8,128)(2,1)S(1)}, bf16[192,4096]{1,0:T(8,128)(2,1)}, u32[]{:S(2)}) copy-start(bf16[192,4096]{1,0:T(8,128)(2,1)} %get-tuple-element.12) | copy-start | bytes 4718596
  237.7 2.0 copy-start.1
  239.7 2.0 copy-start
